TPU v7x, 32 devices: a whole 2x2x4 slice. The times are simulated.
32 devices in a mesh: clu: 8 (over z, y), rhs: 4 (over x, core).
Axes of the slice: x: 2, y: 2, z: 4, core: 2. Of those that a mesh axis runs over, the one named last changes fastest.
Arguments:
- right_side: float32 [64, 4096], P('rhs', 'clu')
- self_term: float32 [4096], P('clu'), may hold values from 3 to 9
- near_pairs: int32 [512, 2], P('clu'), may hold values from 0 to 15, as said below
- near_blocks: bfloat16 [512, 256, 256], P('clu'), may hold values from -0.046875 to 0.046875
- near_scale: float32 [512], P('clu'), may hold values from 0.5 to 1.5
- near_count: int32 [8], P('clu'), may hold values from 16 to 64, as said below
- far_pairs: int32 [512, 2], P('clu'), may hold values from 0 to 15, as said below
- far_left: bfloat16 [512, 32, 256], P('clu'), may hold values from -1 to 1
- far_right: bfloat16 [512, 32, 256], P('clu'), may hold values from -1 to 1
- far_scale: float32 [512], P('clu'), may hold values from 0.03 to 0.1
- far_rank: int32 [512], P('clu'), may hold values from 8 to 32, as said below
- far_count: int32 [8], P('clu'), may hold values from 16 to 64, as said below
Outputs:
- solution: float32 [64, 4096], P('rhs', 'clu')
- residual: float32 [64, 4096], P('rhs', 'clu')
Inputs may be any that keep to these rules, and one draw needn't show every extreme that they name: near_pairs[s, 0] is one of the 2 clusters of the index of clu that holds slot s (s // 64); near_pairs[s, 1] is a cluster of that index or of the index beside it on either side. far_pairs[s, 0] is one of the 2 clusters of the index of clu that holds slot s (s // 64); among the slots of one index of clu, at most 16 have their second cluster on any one index of clu, and some index of clu holds the second cluster of exactly 16 slots of every index. `near_count`: live near slots of each index of clu; slots at or after the count hold blocks that are ignored. `far_count`: live far slots of each index of clu; slots at or after the count hold blocks that are ignored. Only the first far_rank rows of a far block's factors are used.
All inputs are finite; a program needn't handle non-finite values.
Results may differ from a plain program's by a relative error of at most 0.0019.
Values may be sent and summed in bfloat16 or wider, within the bound.
A program may use at most 64 MiB of HBM per device.

v0:
```python
import jax
import jax.numpy as jnp
from jax import lax
from jax.sharding import PartitionSpec as P

CLUSTER = 256
ITERS = 2


PRECISE = lax.Precision.HIGHEST


def near_terms(grid, first_index, second_index, near_blocks, near_weight):
    summed = jnp.zeros(grid.shape, jnp.float32)
    near_first = jnp.take(grid, first_index, axis=1)
    near_second = jnp.take(grid, second_index, axis=1)
    scaling = near_weight[None, :, None]
    toward_first = (
        jnp.einsum("spq,csq->csp", near_blocks, near_second, preferred_element_type=jnp.float32)
        * scaling
    )
    toward_second = (
        jnp.einsum("spq,csp->csq", near_blocks, near_first, preferred_element_type=jnp.float32)
        * scaling
    )
    summed = summed.at[:, first_index].add(toward_first)
    summed = summed.at[:, second_index].add(toward_second)
    return summed


def first_coefs(grid, first_index, far_left, far_weight, keeps):
    far_first = jnp.take(grid, first_index, axis=1)
    coef = (
        jnp.einsum("srp,csp->scr", far_left, far_first, preferred_element_type=jnp.float32)
        * far_weight[:, None, None]
    )
    return jnp.where(keeps[:, None, :], coef, 0.0).astype(jnp.bfloat16)


def build_operator(
    self_term,
    near_pairs,
    near_blocks,
    near_scale,
    near_count,
    far_pairs,
    far_left,
    far_right,
    far_scale,
    far_rank,
    far_count,
):
    near_live = (jnp.arange(near_blocks.shape[0], dtype=jnp.int32) < near_count[0]).astype(
        jnp.float32
    )
    far_live = (jnp.arange(far_left.shape[0], dtype=jnp.int32) < far_count[0]).astype(jnp.float32)
    near_weight = near_scale * near_live
    far_weight = far_scale * far_live
    keeps = jnp.arange(far_left.shape[1], dtype=jnp.int32)[None, :] < far_rank[:, None]

    def operate(charge_field):
        charges = charge_field.astype(jnp.bfloat16)
        gathered = lax.all_gather(charges, "clu", axis=1, tiled=True)
        rows_here = gathered.shape[0]
        grid = gathered.reshape(rows_here, -1, CLUSTER)
        summed = near_terms(grid, near_pairs[:, 0], near_pairs[:, 1], near_blocks, near_weight)
        far_second = jnp.take(grid, far_pairs[:, 1], axis=1)
        coef_second = jnp.einsum(
            "srq,csq->scr", far_right, far_second, preferred_element_type=jnp.float32
        )
        coef_second = jnp.where(keeps[:, None, :], coef_second, 0.0).astype(jnp.bfloat16)
        coef_first = first_coefs(grid, far_pairs[:, 0], far_left, far_weight, keeps)
        toward_first = (
            jnp.einsum("srp,scr->csp", far_left, coef_second, preferred_element_type=jnp.float32)
            * far_weight[None, :, None]
        )
        toward_second = jnp.einsum(
            "srq,scr->csq", far_right, coef_first, preferred_element_type=jnp.float32
        )
        summed = summed.at[:, far_pairs[:, 0]].add(toward_first)
        summed = summed.at[:, far_pairs[:, 1]].add(toward_second)
        reduced = lax.psum_scatter(
            summed.reshape(rows_here, -1), "clu", scatter_dimension=1, tiled=True
        )
        return self_term[None, :] * charge_field + reduced

    return operate


def solve_spd(matrix, target):
    return jax.scipy.linalg.cho_solve((jnp.linalg.cholesky(matrix), True), target)


def shards(
    right_side,
    self_term,
    near_pairs,
    near_blocks,
    near_scale,
    near_count,
    far_pairs,
    far_left,
    far_right,
    far_scale,
    far_rank,
    far_count,
):
    operate = build_operator(
        self_term,
        near_pairs,
        near_blocks,
        near_scale,
        near_count,
        far_pairs,
        far_left,
        far_right,
        far_scale,
        far_rank,
        far_count,
    )
    group_width = right_side.shape[0]

    def gram_columns(left_rows, right_rows):
        return lax.psum(jnp.dot(left_rows, right_rows.T, precision=PRECISE), "clu")

    def residual_gram(current):
        every_column = lax.all_gather(current, "rhs", axis=0, tiled=True)
        return gram_columns(every_column, every_column)

    def own_columns(matrix):
        return lax.dynamic_slice_in_dim(matrix, lax.axis_index("rhs") * group_width, group_width, 1)

    solution = jnp.zeros_like(right_side)
    residual = right_side
    direction = right_side
    norms = residual_gram(residual)
    for step in range(ITERS):
        image = operate(direction)
        direction_all, image_all = (
            lax.all_gather(direction, "rhs", axis=0, tiled=True),
            lax.all_gather(image, "rhs", axis=0, tiled=True),
        )
        curvature = gram_columns(direction_all, image_all)
        alpha_own = own_columns(solve_spd(curvature, norms))
        solution = solution + jnp.dot(alpha_own.T, direction_all, precision=PRECISE)
        residual = residual - jnp.dot(alpha_own.T, image_all, precision=PRECISE)
        if step + 1 < ITERS:
            norms_next = residual_gram(residual)
            beta_own = own_columns(solve_spd(norms, norms_next))
            direction = residual + jnp.dot(beta_own.T, direction_all, precision=PRECISE)
            norms = norms_next
    return (solution, residual)


def solution(mesh):
    placed = (
        P("rhs", "clu"),
        P("clu"),
        P("clu", None),
        P("clu", None, None),
        P("clu"),
        P("clu"),
        P("clu", None),
        P("clu", None, None),
        P("clu", None, None),
        P("clu"),
        P("clu"),
        P("clu"),
    )
    return jax.shard_map(
        shards,
        mesh=mesh,
        in_specs=placed,
        out_specs=(P("rhs", "clu"), P("rhs", "clu")),
        check_vma=False,
    )
```

profile of v0, /device:TPU:0, one launch (start us, length us, event | category | flops | bytes accessed | tf_op | source)
XLA Modules:
  0.0 450.7 jit_solution(3501696170188582463)
XLA Ops:
  9.6 32.3 %all_gather.22 = bf16[16,4096]{1,0:T(8,128)(2,1)S(1)} all-gather(bf16[16,512]{1,0:T(8,128)(2,1)S(1)} %convert_element_type.20), channel_id=1, replica_groups=mesh['clu'=8,'rhs'=4] {'clu'}, dimensions={1}, use_global_device_ids=true | all-gather | bytes 147456 | tf_op jit(solution)/shard_map/all_gather | solution.py:63
  49.6 7.0 %convolution_multiply_fusion.3 = f32[64,16,256]{2,1,0:T(8,128)} fusion(bf16[64,256,256]{2,1,0:T(8,128)(2,1)} %param.20, bf16[64,16,256]{2,1,0:T(8,128)(2,1)S(1)} %gather_fusion, f32[64]{0:T(128)S(1)} %compare_select_fusion.9, pred[64]{0:T(512)(128)(4,1)S(1)} %get-tuple-element.25), kind=kOutput, calls=%fused_computation.19 | convolution fusion | flops 134742016 | bytes 9961792 | tf_op jit(solution)/shard_map/spq,csq->csp/dot_general | solution.py:19
  63.3 6.2 %scatter_fusion = f32[16,16,256]{2,0,1:T(8,128)S(1)} fusion(f32[16,16,256]{2,0,1:T(8,128)S(1)} %broadcast.91.clone, s32[64]{0:T(128)S(1)} %get-tuple-element.22, f32[64,16,256]{2,1,0:T(8,128)} %convolution_multiply_fusion.3), kind=kCustom, calls=%fused_computation.8 | custom fusion | flops 262144 | bytes 3145984 | tf_op jit(solution)/shard_map/scatter-add | solution.py:26
  72.7 6.2 %scatter_fusion.2 = f32[16,16,256]{2,0,1:T(8,128)S(1)} fusion(f32[16,16,256]{2,0,1:T(8,128)S(1)} %scatter_fusion.1, s32[64]{0:T(128)S(1)} %get-tuple-element.29, f32[64,16,256]{2,1,0:T(8,128)} %convolution_multiply_fusion.5), kind=kCustom, calls=%fused_computation.10 | custom fusion | flops 262144 | bytes 3145984 | tf_op jit(solution)/shard_map/scatter-add | solution.py:80
  78.9 6.2 %scatter_fusion.3 = f32[16,16,256]{2,0,1:T(8,128)S(1)} fusion(f32[16,16,256]{2,0,1:T(8,128)S(1)} %scatter_fusion.2, s32[64]{0:T(128)S(1)} %get-tuple-element.30, f32[64,16,256]{2,1,0:T(8,128)} %fusion.6), kind=kCustom, calls=%fused_computation.11 | custom fusion | flops 262144 | bytes 3145984 | tf_op jit(solution)/shard_map/scatter-add | solution.py:81
  85.9 5.4 %all_gather.24 = f32[64,512]{1,0:T(8,128)S(1)} all-gather(f32[16,512]{1,0:T(8,128)S(1)} %copy-done.5), channel_id=1, replica_groups=mesh['clu'=8,'rhs'=4] {'rhs'}, dimensions={0}, use_global_device_ids=true | all-gather | bytes 163840 | tf_op jit(solution)/shard_map/all_gather | solution.py:140
  91.6 56.6 %reduce-scatter.3.cloned.1.call-done = f32[16,512]{1,0:T(8,128)} async-done(((f32[16,4096]{1,0:T(8,128)}), f32[16,512]{1,0:T(8,128)}) %reduce-scatter.3.cloned.1.call-update) | async-done | bytes 32784 | tf_op jit(solution)/shard_map/reduce_scatter | solution.py:82
  148.9 5.4 %all_gather.23 = f32[64,512]{1,0:T(8,128)S(1)} all-gather(f32[16,512]{1,0:T(8,128)S(1)} %multiply_add_fusion.1), channel_id=1, replica_groups=mesh['clu'=8,'rhs'=4] {'rhs'}, dimensions={0}, use_global_device_ids=true | all-gather | bytes 163840 | tf_op jit(solution)/shard_map/all_gather | solution.py:141
  154.6 35.6 %all-reduce = (f32[64,64]{0,1:T(8,128)S(1)}, f32[64,64]{0,1:T(8,128)S(1)}) all-reduce(f32[64,64]{0,1:T(8,128)S(1)} %fusion.116, f32[64,64]{0,1:T(8,128)S(1)} %convolution_bitcast_fusion), channel_id=1, replica_groups=mesh['clu'=8,'rhs'=4] {'clu'}, use_global_device_ids=true, to_apply=%region_8.11 | all-reduce | flops 8192 | bytes 65536 | tf_op jit(solution)/shard_map/psum | solution.py:124
  190.3 5.8 %cholesky.70 = f32[64,64]{1,0:T(8,128)S(1)} custom-call(f32[64,64]{1,0:T(8,128)S(1)} %fusion.78), custom_call_target="Cholesky" | custom-call | tf_op jit(solution)/shard_map/jit(cholesky)/cholesky | solution.py:91
  197.5 4.9 %custom-call.10 = f32[1,64,64]{1,2,0:T(8,128)S(1)} custom-call(f32[1,64,64]{2,1,0:T(8,128)S(1)} %fusion.67), custom_call_target="InvertDiagBlocksLowerTriangular" | custom-call | tf_op jit(solution)/shard_map/jit(_cho_solve)/triangular_solve | solution.py:91
  202.5 5.8 %cholesky.59 = f32[64,64]{1,0:T(8,128)S(1)} custom-call(f32[64,64]{1,0:T(8,128)S(1)} %fusion.83), custom_call_target="Cholesky" | custom-call | tf_op jit(solution)/shard_map/jit(cholesky)/cholesky | solution.py:91
  215.3 5.4 %all_gather.25 = f32[64,512]{1,0:T(8,128)S(1)} all-gather(f32[16,512]{1,0:T(8,128)S(1)} %convolution_subtract_fusion.1), channel_id=1, replica_groups=mesh['clu'=8,'rhs'=4] {'rhs'}, dimensions={0}, use_global_device_ids=true | all-gather | bytes 163840 | tf_op jit(solution)/shard_map/all_gather | solution.py:127
  221.0 33.0 %psum.30 = f32[64,64]{1,0:T(8,128)S(1)} all-reduce(f32[64,64]{1,0:T(8,128)S(1)} %fusion.117), channel_id=1, replica_groups=mesh['clu'=8,'rhs'=4] {'clu'}, use_global_device_ids=true, to_apply=%region_9.13 | all-reduce | flops 4096 | bytes 32768 | tf_op jit(solution)/shard_map/psum | solution.py:124
  254.7 30.5 %all_gather.27 = bf16[16,4096]{1,0:T(8,128)(2,1)S(1)} all-gather(bf16[16,512]{1,0:T(8,128)(2,1)S(1)} %get-tuple-element.23), channel_id=1, replica_groups=mesh['clu'=8,'rhs'=4] {'clu'}, dimensions={1}, use_global_device_ids=true | all-gather | bytes 147456 | tf_op jit(solution)/shard_map/all_gather | solution.py:63
  290.0 6.7 %convolution_multiply_fusion.1 = f32[64,16,256]{2,1,0:T(8,128)} fusion(bf16[64,256,256]{2,1,0:T(8,128)(2,1)} %param.20, bf16[64,16,256]{2,1,0:T(8,128)(2,1)S(1)} %gather_fusion.4, f32[64]{0:T(128)S(1)} %compare_select_fusion.9, pred[64]{0:T(512)(128)(4,1)S(1)} %get-tuple-element.25), kind=kOutput, calls=%fused_computation.17 | convolution fusion | flops 134742016 | bytes 9961792 | tf_op jit(solution)/shard_map/spq,csq->csp/dot_general | solution.py:19
  306.8 6.2 %scatter_fusion.4 = f32[16,16,256]{2,0,1:T(8,128)S(1)} fusion(f32[16,16,256]{2,0,1:T(8,128)S(1)} %broadcast.91, s32[64]{0:T(128)S(1)} %get-tuple-element.22, f32[64,16,256]{2,1,0:T(8,128)} %convolution_multiply_fusion.1), kind=kCustom, calls=%fused_computation.12 | custom fusion | flops 262144 | bytes 3145984 | tf_op jit(solution)/shard_map/scatter-add | solution.py:26
  316.2 6.2 %scatter_fusion.6 = f32[16,16,256]{2,0,1:T(8,128)S(1)} fusion(f32[16,16,256]{2,0,1:T(8,128)S(1)} %scatter_fusion.5, s32[64]{0:T(128)S(1)} %get-tuple-element.29, f32[64,16,256]{2,1,0:T(8,128)} %convolution_multiply_fusion.4), kind=kCustom, calls=%fused_computation.14 | custom fusion | flops 262144 | bytes 3145984 | tf_op jit(solution)/shard_map/scatter-add | solution.py:80
  322.4 6.2 %scatter_fusion.7 = f32[16,16,256]{2,0,1:T(8,128)S(1)} fusion(f32[16,16,256]{2,0,1:T(8,128)S(1)} %scatter_fusion.6, s32[64]{0:T(128)S(1)} %get-tuple-element.30, f32[64,16,256]{2,1,0:T(8,128)} %fusion.7), kind=kCustom, calls=%fused_computation.15 | custom fusion | flops 262144 | bytes 3145984 | tf_op jit(solution)/shard_map/scatter-add | solution.py:81
  329.3 5.6 %all_gather.26 = f32[64,512]{1,0:T(8,128)S(1)} all-gather(f32[16,512]{1,0:T(8,128)S(1)} %get-tuple-element.24), channel_id=1, replica_groups=mesh['clu'=8,'rhs'=4] {'rhs'}, dimensions={0}, use_global_device_ids=true | all-gather | bytes 163840 | tf_op jit(solution)/shard_map/all_gather | solution.py:140
  335.2 52.8 %reduce-scatter.5.cloned.1.call-done = f32[16,512]{1,0:T(8,128)} async-done(((f32[16,4096]{1,0:T(8,128)}), f32[16,512]{1,0:T(8,128)}) %reduce-scatter.5.cloned.1.call-update) | async-done | bytes 32784 | tf_op jit(solution)/shard_map/reduce_scatter | solution.py:82
  388.8 5.4 %all_gather.28 = f32[64,512]{1,0:T(8,128)S(1)} all-gather(f32[16,512]{1,0:T(8,128)S(1)} %multiply_add_fusion), channel_id=1, replica_groups=mesh['clu'=8,'rhs'=4] {'rhs'}, dimensions={0}, use_global_device_ids=true | all-gather | bytes 163840 | tf_op jit(solution)/shard_map/all_gather | solution.py:141
  394.4 35.2 %psum.31 = f32[64,64]{0,1:T(8,128)S(1)} all-reduce(f32[64,64]{0,1:T(8,128)S(1)} %fusion.118), channel_id=1, replica_groups=mesh['clu'=8,'rhs'=4] {'clu'}, use_global_device_ids=true, to_apply=%region_15.19 | all-reduce | flops 4096 | bytes 32768 | tf_op jit(solution)/shard_map/psum | solution.py:124
  429.7 5.8 %cholesky.81 = f32[64,64]{1,0:T(8,128)S(1)} custom-call(f32[64,64]{1,0:T(8,128)S(1)} %fusion.73), custom_call_target="Cholesky" | custom-call | tf_op jit(solution)/shard_map/jit(cholesky)/cholesky | solution.py:91
  (86 shorter events, 58.3 us)
Async XLA Ops:
  7.2 50.7 %copy-start = (bf16[64,32,256]{2,1,0:T(8,128)(2,1)S(1)}, bf16[64,32,256]{2,1,0:T(8,128)(2,1)}, u32[]{:S(2)}) copy-start(bf16[64,32,256]{2,1,0:T(8,128)(2,1)} %param.24) | copy-start | bytes 3145732
  7.2 141.0 %reduce-scatter.3.cloned.1.call-start = ((), (), s32[]{:S(2)}) async-start(), calls=%async_computation.2 | async-start | bytes 294912 | tf_op jit(solution)/shard_map/reduce_scatter | solution.py:82
  48.7 7.8 %copy-start.1 = (bf16[64,256,256]{2,1,0:T(8,128)(2,1)S(1)}, bf16[64,256,256]{2,1,0:T(8,128)(2,1)}, u32[]{:S(2)}) copy-start(bf16[64,256,256]{2,1,0:T(8,128)(2,1)} %param.20) | copy-start | bytes 25165828
  48.8 7.8 %copy-start.3 = (bf16[64,16,256]{2,1,0:T(8,128)(2,1)S(1)}, bf16[64,16,256]{2,1,0:T(8,128)(2,1)}, u32[]{:S(2)}) copy-start(bf16[64,16,256]{2,1,0:T(8,128)(2,1)} %gather_fusion.1) | copy-start | bytes 1572868
  56.6 1.3 copy-start.7
  56.6 1.3 copy-start.2
  60.6 25.3 %copy-start.5 = (f32[16,512]{1,0:T(8,128)S(1)}, f32[16,512]{1,0:T(8,128)}, u32[]{:S(2)}) copy-start(f32[16,512]{1,0:T(8,128)} %param.17) | copy-start | bytes 98308
  60.6 87.6 %copy-start.6 = (f32[512]{0:T(512)S(1)}, f32[512]{0:T(512)}, u32[]{:S(2)}) copy-start(f32[512]{0:T(512)} %param.18) | copy-start | bytes 6148
  85.8 302.2 %reduce-scatter.5.cloned.1.call-start = ((), (), s32[]{:S(2)}) async-start(), calls=%async_computation.3 | async-start | bytes 294912 | tf_op jit(solution)/shard_map/reduce_scatter | solution.py:82
  290.0 6.7 %copy-start.4 = (bf16[64,16,256]{2,1,0:T(8,128)(2,1)S(1)}, bf16[64,16,256]{2,1,0:T(8,128)(2,1)}, u32[]{:S(2)}) copy-start(bf16[64,16,256]{2,1,0:T(8,128)(2,1)} %gather_fusion.5) | copy-start | bytes 1572868
Sparse Core Ops, SparseCore 0:
  86.0 62.1 reduce-scatter.2
  329.5 58.4 reduce-scatter.4
where the time goes:
time: 452 us; the launch traced here: 451 us
  blocking collectives  194 us (43%)
  waiting for transfers between devices  109 us (24%)
  other arithmetic  85.3 us (19%)
  matrix products  34.9 us (8%)
  between operations  15.7 us (3%)
  local copies, waits for them, and re-layouts  11.3 us (2%)
    reduce_scatter x2, waiting for transfers between devices, operate(): lax.psum_scatter(summed.reshape(rows_here, -1), 'clu', scatter_dimension=...  109 us
    psum x3, blocking collectives, gram_columns(): return lax.psum(jnp.dot(left_rows, right_rows.T, precision=PRECISE), 'clu')  104 us
    all_gather x2, blocking collectives, operate(): gathered = lax.all_gather(charges, 'clu', axis=1, tiled=True)  62.8 us
    another operation x9, other arithmetic, solve_spd(): jnp.linalg.cholesky(matrix)  19.6 us
    another operation x6, other arithmetic, solve_spd(): jax.scipy.linalg.cho_solve((jnp.linalg.cholesky(matrix), True), target)  16.6 us
    dot_general x2, matrix products, near_terms(): jnp.einsum('spq,csq->csp', near_blocks, near_second, preferred_element_ty...  13.8 us
    scatter-add x2, other arithmetic, near_terms(): summed = summed.at[:, first_index].add(toward_first)  12.4 us
    scatter-add x2, other arithmetic, operate(): summed = summed.at[:, far_pairs[:, 0]].add(toward_first)  12.4 us
  transfers between devices with their start and end apart: 2, of which 2 were waited for; matrix products, arithmetic and copies ran while one was open for 0% of the time, Pallas kernels for 0%

commit v1 on v0

v1 whole, which is shorter than its diff:
```python
import functools

import jax
import jax.numpy as jnp
from jax import lax
from jax.experimental import pallas as pl
from jax.experimental.pallas import tpu as pltpu
from jax.sharding import PartitionSpec as P

CLUSTER = 256
PRECISE = lax.Precision.HIGHEST
F32 = jnp.float32
BF16 = jnp.bfloat16
MESH = pl.DeviceIdType.MESH

NT = (((1,), (1,)), ((), ()))
NN = (((1,), (0,)), ((), ()))
TN = (((0,), (0,)), ((), ()))


def dot(left, right, dims):
    return lax.dot_general(left, right, dims, preferred_element_type=F32)


def exact(left, right, dims):
    return lax.dot_general(left, right, dims, precision=PRECISE, preferred_element_type=F32)


def solve_many(systems):
    size, wide = systems[0].shape
    step = 8
    row_at = lax.broadcasted_iota(jnp.int32, (size, 1), 0)

    def block(_, current):
        current = list(current)
        for k in range(step):
            for at, m in enumerate(current):
                column = m[:, k : k + 1]
                row = m[k : k + 1, :] * (1.0 / m[k : k + 1, k : k + 1])
                current[at] = jnp.where(row_at == k, row, m - column * row)
        return tuple(
            pltpu.roll(jnp.concatenate([m[step:], m[:step]], axis=0), wide - step, 1)
            for m in current
        )

    done = lax.fori_loop(0, size // step, block, tuple(systems))
    return [m[:, : wide - size] for m in done]


def kernel(
    sizes,
    right_ref,
    self_ref,
    near_pairs,
    near_scale,
    near_count,
    far_pairs,
    far_scale,
    far_rank,
    far_count,
    near_hbm,
    left_hbm,
    rightf_hbm,
    solution_ref,
    residual_ref,
    near,
    far_l,
    far_r,
    meta_i,
    meta_j,
    meta_keep,
    meta_w,
    lhs,
    grid,
    around,
    sums,
    parts,
    slabs,
    all_right,
    all_image,
    all_direction,
    all_residual,
    grams,
    first_solution,
    load_sem,
    clu_send,
    clu_recv,
    rhs_send,
    rhs_recv,
):
    n_clu, n_rhs, rows, near_slots, far_slots, rank = sizes
    me, col = lax.axis_index("clu"), lax.axis_index("rhs")
    n_cl = 2 * n_clu
    own = pl.ds(pl.multiple_of(col * rows, rows), rows)
    own_block = pl.ds(pl.multiple_of(me * 2 * rows, 2 * rows), 2 * rows)
    tile = 256
    slots_tile = tile // rank
    tiles = far_slots // slots_tile
    group = 4

    def near_load(g):
        part = pl.ds(g * (near_slots // group), near_slots // group)
        return pltpu.make_async_copy(near_hbm.at[part], near.at[part], load_sem.at[2 + g])

    loads = [
        pltpu.make_async_copy(left_hbm, far_l, load_sem.at[0]),
        pltpu.make_async_copy(rightf_hbm, far_r, load_sem.at[1]),
    ] + [near_load(g) for g in range(group)]
    for load in loads:
        load.start()

    barrier = pltpu.get_barrier_semaphore()

    @pl.loop(1, n_clu)
    def _(d):
        pl.semaphore_signal(
            barrier, inc=1, device_id={"clu": lax.rem(me + d, n_clu)}, device_id_type=MESH
        )

    for d in range(1, n_rhs):
        pl.semaphore_signal(
            barrier, inc=1, device_id={"rhs": lax.rem(col + d, n_rhs)}, device_id_type=MESH
        )

    def clu_copy(kind, d, src, dst):
        return pltpu.make_async_remote_copy(
            src_ref=src,
            dst_ref=dst,
            send_sem=clu_send.at[kind, d],
            recv_sem=clu_recv.at[kind, d],
            device_id={"clu": lax.rem(me + d, n_clu)},
            device_id_type=MESH,
        )

    def rhs_copy(kind, d, ref):
        return pltpu.make_async_remote_copy(
            src_ref=ref.at[own],
            dst_ref=ref.at[own],
            send_sem=rhs_send.at[kind, d],
            recv_sem=rhs_recv.at[kind, d],
            device_id={"rhs": lax.rem(col + d, n_rhs)},
            device_id_type=MESH,
        )

    def rhs_start(kind, ref):
        for d in range(1, n_rhs):
            rhs_copy(kind, d, ref).start()

    def rhs_wait(kind, ref):
        for d in range(1, n_rhs):
            rhs_copy(kind, d, ref).wait()

    def grid_copy(it, d):
        block = grid.at[it, own_block]
        return clu_copy(it, d, block, block)

    def slab_copy(which, d):
        block = slabs.at[which, me]
        return clu_copy(4 + which, d, block, block)

    def sums_copy(it, d):
        there = lax.rem(me + d, n_clu)
        src = sums.at[it, pl.ds(pl.multiple_of(there * 2 * rows, 2 * rows), 2 * rows)]
        return clu_copy(2 + it, d, src, parts.at[it, me])

    def start_all(copy, which):
        @pl.loop(1, n_clu)
        def _(d):
            copy(which, d).start()

    def wait_all(copy, which):
        @pl.loop(1, n_clu)
        def _(d):
            copy(which, d).wait()

    def set_charges(it, field):
        grid[it, own_block] = jnp.concatenate(
            [field[:, :CLUSTER], field[:, CLUSTER:]], axis=0
        ).astype(BF16)

    def slab_sum(which):
        return lax.fori_loop(
            1, n_clu, lambda k, total: total + slabs[which, k], slabs[which, 0]
        )

    field = right_ref[...]
    set_charges(0, field)
    all_right[own] = field
    pl.semaphore_wait(barrier, n_clu + n_rhs - 2)
    start_all(grid_copy, 0)
    rhs_start(0, all_right)

    lane = lax.broadcasted_iota(jnp.int32, (1, 128), 1)
    slot_in = lane // rank
    live = far_count[0]
    per = 128 // rank
    for g in range(far_slots // per):
        at = slice(g * 128, (g + 1) * 128)

        def spread(value):
            out = jnp.full((1, 128), value(g * per))
            for q in range(1, per):
                out = jnp.where(slot_in == q, value(g * per + q), out)
            return out

        meta_i[:, at] = spread(lambda s: far_pairs[s, 0])
        meta_j[:, at] = spread(lambda s: far_pairs[s, 1])
        meta_keep[:, at] = jnp.where(
            lane - slot_in * rank < spread(lambda s: far_rank[s]), 1.0, 0.0
        )
        meta_w[:, at] = spread(
            lambda s: jnp.where(s < live, far_scale[s], jnp.zeros((), F32))
        )

    rhs_wait(0, all_right)
    blank = jnp.zeros((rows, 128 - n_rhs * rows), F32)
    slabs[0, me] = jnp.concatenate([exact(all_right[own], all_right[...], NT), blank], axis=1)
    start_all(slab_copy, 0)

    def apply(it, field):
        first_far = jnp.zeros((4 * rows, CLUSTER), F32)
        for t in range(tiles):
            at = slice(t * tile, (t + 1) * tile)
            right_tile, left_tile = far_r[at, :], far_l[at, :]
            to_i, to_j = meta_i[:, at], meta_j[:, at]
            keep, weight = meta_keep[:, at], meta_w[:, at]

            def pick(b, coef):
                base = pl.multiple_of(b * 16 * rows, 16 * rows)
                product = dot(grid[it, pl.ds(base, 16 * rows)], right_tile, NT)
                for q in range(16):
                    coef = coef + jnp.where(
                        to_j == b * 16 + q, product[q * rows : (q + 1) * rows], 0.0
                    )
                return coef

            coef_second = jnp.zeros((rows, tile), F32)
            if n_cl == 16:
                coef_second = pick(0, coef_second)
            else:
                coef_second = lax.fori_loop(0, n_cl // 16, pick, coef_second)
            coef_second = jnp.where(keep > 0.0, coef_second, 0.0).astype(BF16).astype(F32) * weight
            high = coef_second.astype(BF16).astype(F32)
            low = coef_second - high
            low_cluster = to_i == 2 * me
            stack = jnp.concatenate(
                [
                    jnp.where(low_cluster, high, 0.0),
                    jnp.where(low_cluster, 0.0, high),
                    jnp.where(low_cluster, low, 0.0),
                    jnp.where(low_cluster, 0.0, low),
                ],
                axis=0,
            ).astype(BF16)
            first_far = first_far + dot(stack, left_tile, NN)
            both = dot(grid[it, own_block], left_tile, NT)
            coef_first = jnp.where(low_cluster, both[:rows], both[rows:]) * weight
            coef_first = jnp.where(keep > 0.0, coef_first, 0.0)

            def spread_rows(b, carry):
                for q in range(16):
                    base = pl.multiple_of(b * 16 * rows + q * rows, rows)
                    lhs[pl.ds(base, rows), at] = jnp.where(
                        to_j == b * 16 + q, coef_first, 0.0
                    ).astype(BF16)
                return carry

            if n_cl == 16:
                spread_rows(0, 0)
            else:
                lax.fori_loop(0, n_cl // 16, spread_rows, 0)

        def second_far(b, carry):
            part = pl.ds(pl.multiple_of(b * 16 * rows, 16 * rows), 16 * rows)
            sums[it, part] = dot(lhs[part], far_r[...], NN)
            return carry

        lax.fori_loop(0, n_cl // 16, second_far, 0)

        @pl.loop(2, n_clu - 1)
        def _(d):
            sums_copy(it, d).start()

        for side, there in enumerate((me + n_clu - 1, me, me + 1)):
            base = pl.multiple_of(lax.rem(there, n_clu) * 2 * rows, 2 * rows)
            around[side * 2 * rows : (side + 1) * 2 * rows] = grid[
                it, pl.ds(base, 2 * rows)
            ].astype(F32)
        near_live = near_count[0]
        unroll = 4
        zero = jnp.zeros((rows, CLUSTER), F32)

        def near_slots_step(g, carry):
            carry = list(carry)
            for u in range(unroll):
                s = g * unroll + u
                i, j = near_pairs[s, 0], near_pairs[s, 1]
                weight = jnp.where(s < near_live, near_scale[s], jnp.zeros((), F32))
                block = near[s]
                offset = j - 2 * me + 2
                offset = jnp.where(offset < 0, offset + n_cl, offset)
                offset = jnp.where(offset >= n_cl, offset - n_cl, offset)
                is_first = [jnp.where(i - 2 * me == q, 1.0, 0.0) for q in range(2)]
                is_second = [jnp.where(offset == q, 1.0, 0.0) for q in range(6)]
                first = is_first[0] * around[2 * rows : 3 * rows]
                first = first + is_first[1] * around[3 * rows : 4 * rows]
                second = is_second[0] * around[:rows]
                for q in range(1, 6):
                    second = second + is_second[q] * around[q * rows : (q + 1) * rows]
                toward_first = dot(second.astype(BF16), block, NT)
                toward_second = dot(first.astype(BF16), block, NN)
                for q in range(2):
                    carry[q] = carry[q] + (is_first[q] * weight) * toward_first
                for q in range(6):
                    carry[2 + q] = carry[2 + q] + (is_second[q] * weight) * toward_second
            return tuple(carry)

        carry = (zero,) * 8
        steps = near_slots // unroll // group
        for g in range(group):
            if it == 0:
                near_load(g).wait()
            carry = lax.fori_loop(g * steps, (g + 1) * steps, near_slots_step, carry)
        for side, there in enumerate((me + n_clu - 1, me, me + 1)):
            base = pl.multiple_of(lax.rem(there, n_clu) * 2 * rows, 2 * rows)
            pair = jnp.concatenate([carry[2 + 2 * side], carry[3 + 2 * side]], axis=0)
            if side == 1:
                pair = pair + jnp.concatenate([carry[0], carry[1]], axis=0)
                pair = pair + first_far[: 2 * rows] + first_far[2 * rows :]
            sums[it, pl.ds(base, 2 * rows)] += pair
        sums_copy(it, 1).start()
        sums_copy(it, n_clu - 1).start()
        wait_all(sums_copy, it)
        total = sums[it, own_block]

        def add(d, total):
            return total + parts[it, lax.rem(me + d, n_clu)]

        total = lax.fori_loop(1, n_clu, add, total)
        return self_ref[...] * field + jnp.concatenate([total[:rows], total[rows:]], axis=1)

    wait_all(grid_copy, 0)
    loads[0].wait()
    loads[1].wait()
    image = apply(0, field)
    all_image[0, own] = image
    rhs_start(1, all_image.at[0])
    rhs_wait(1, all_image.at[0])
    slabs[1, me] = jnp.concatenate(
        [exact(image, all_image[0], NT), exact(image, all_right[...], NT)], axis=1
    )
    start_all(slab_copy, 1)
    wait_all(slab_copy, 0)
    wait_all(slab_copy, 1)
    grams[0, own] = jnp.concatenate([slab_sum(1), slab_sum(0)], axis=1)
    rhs_start(2, grams.at[0])
    rhs_wait(2, grams.at[0])

    count = n_rhs * rows
    together = grams[0]
    image_image = together[:, :count]
    image_right = together[:, count : 2 * count]
    norms = together[:, 128 : 128 + count]
    right_image = image_right.T
    curvature = 0.5 * (image_right + right_image)
    identity = jnp.where(
        lax.broadcasted_iota(jnp.int32, (count, count), 0)
        == lax.broadcasted_iota(jnp.int32, (count, count), 1),
        1.0,
        0.0,
    )
    alpha, inverse = solve_many(
        [
            jnp.concatenate([curvature, norms], axis=1),
            jnp.concatenate([norms, identity], axis=1),
        ]
    )
    crossed = exact(right_image, alpha, NN)
    next_norms = norms - crossed - crossed.T
    next_norms = next_norms + exact(alpha, exact(image_image, alpha, NN), TN)
    beta = exact(inverse, next_norms, NN)
    all_residual[...] = all_right[...] - exact(alpha, all_image[0], TN)
    all_direction[...] = all_residual[...] + exact(beta, all_right[...], TN)
    field = all_direction[own]
    set_charges(1, field)
    start_all(grid_copy, 1)
    slabs[2, me] = jnp.concatenate(
        [exact(all_residual[own], all_residual[...], NT), blank], axis=1
    )
    start_all(slab_copy, 2)
    first_solution[...] = exact(alpha, all_right[...], TN)
    wait_all(grid_copy, 1)
    image = apply(1, field)
    all_image[1, own] = image
    rhs_start(3, all_image.at[1])
    rhs_wait(3, all_image.at[1])
    slabs[3, me] = jnp.concatenate(
        [exact(all_direction[own], all_image[1], NT), blank], axis=1
    )
    start_all(slab_copy, 3)
    wait_all(slab_copy, 2)
    wait_all(slab_copy, 3)
    grams[1, own] = jnp.concatenate([slab_sum(3), slab_sum(2)], axis=1)
    rhs_start(4, grams.at[1])
    rhs_wait(4, grams.at[1])
    together = grams[1]
    curvature = together[:, :count]
    curvature = 0.5 * (curvature + curvature.T)
    (alpha,) = solve_many(
        [jnp.concatenate([curvature, together[:, 128 : 128 + count]], axis=1)]
    )
    first_solution[...] += exact(alpha, all_direction[...], TN)
    all_residual[...] = all_residual[...] - exact(alpha, all_image[1], TN)
    solution_ref[...] = first_solution[own]
    residual_ref[...] = all_residual[own]


def shards(
    mesh,
    right_side,
    self_term,
    near_pairs,
    near_blocks,
    near_scale,
    near_count,
    far_pairs,
    far_left,
    far_right,
    far_scale,
    far_rank,
    far_count,
):
    n_clu, n_rhs = mesh.shape["clu"], mesh.shape["rhs"]
    rows, width = right_side.shape
    near_slots = near_blocks.shape[0]
    far_slots, rank, _ = far_left.shape
    n_cl = 2 * n_clu
    count = rows * n_rhs
    far_rows = far_slots * rank
    vmem = pl.BlockSpec(memory_space=pltpu.VMEM)
    smem = pl.BlockSpec(memory_space=pltpu.SMEM)
    anywhere = pl.BlockSpec(memory_space=pl.ANY)
    field = jax.ShapeDtypeStruct((rows, width), F32)
    return pl.pallas_call(
        functools.partial(kernel, (n_clu, n_rhs, rows, near_slots, far_slots, rank)),
        out_shape=(field, field),
        in_specs=[vmem, vmem] + [smem] * 7 + [anywhere] * 3,
        out_specs=(vmem, vmem),
        scratch_shapes=[
            pltpu.VMEM(near_blocks.shape, BF16),
            pltpu.VMEM((far_rows, CLUSTER), BF16),
            pltpu.VMEM((far_rows, CLUSTER), BF16),
            pltpu.VMEM((1, far_rows), jnp.int32),
            pltpu.VMEM((1, far_rows), jnp.int32),
            pltpu.VMEM((1, far_rows), F32),
            pltpu.VMEM((1, far_rows), F32),
            pltpu.VMEM((n_cl * rows, far_rows), BF16),
            pltpu.VMEM((2, n_cl * rows, CLUSTER), BF16),
            pltpu.VMEM((6 * rows, CLUSTER), F32),
            pltpu.VMEM((2, n_cl * rows, CLUSTER), F32),
            pltpu.VMEM((2, n_clu, 2 * rows, CLUSTER), F32),
            pltpu.VMEM((4, n_clu, rows, 128), F32),
            pltpu.VMEM((count, width), F32),
            pltpu.VMEM((2, count, width), F32),
            pltpu.VMEM((count, width), F32),
            pltpu.VMEM((count, width), F32),
            pltpu.VMEM((2, count, 256), F32),
            pltpu.VMEM((count, width), F32),
            pltpu.SemaphoreType.DMA((6,)),
            pltpu.SemaphoreType.DMA((8, n_clu)),
            pltpu.SemaphoreType.DMA((8, n_clu)),
            pltpu.SemaphoreType.DMA((5, n_rhs)),
            pltpu.SemaphoreType.DMA((5, n_rhs)),
        ],
        compiler_params=pltpu.CompilerParams(
            collective_id=0, has_side_effects=True, vmem_limit_bytes=48 * 1024 * 1024
        ),
        name="block_cg",
    )(
        right_side,
        self_term.reshape(1, width),
        near_pairs,
        near_scale,
        near_count,
        far_pairs,
        far_scale,
        far_rank,
        far_count,
        near_blocks,
        far_left.reshape(far_rows, CLUSTER),
        far_right.reshape(far_rows, CLUSTER),
    )


def solution(mesh):
    placed = (
        P("rhs", "clu"),
        P("clu"),
        P("clu", None),
        P("clu", None, None),
        P("clu"),
        P("clu"),
        P("clu", None),
        P("clu", None, None),
        P("clu", None, None),
        P("clu"),
        P("clu"),
        P("clu"),
    )
    return jax.shard_map(
        functools.partial(shards, mesh),
        mesh=mesh,
        in_specs=placed,
        out_specs=(P("rhs", "clu"), P("rhs", "clu")),
        check_vma=False,
    )
```

time: 452 us -> 87.1 us (0.19)
  blocking collectives: 194 us -> 0 us
  waiting for transfers between devices: 109 us -> 0 us
  other arithmetic: 85.3 us -> 0 us
  Pallas kernels: 0 us -> 76.1 us
  matrix products: 34.9 us -> 0 us
  between operations: 15.7 us -> 1.94 us
    reduce_scatter x2 -> x0, waiting for transfers between devices: 109 us -> none  [operate(): lax.psum_scatter(summed.reshape(rows_here, -1), 'clu', scatter_dimension=...]
    psum x3 -> x0, blocking collectives: 104 us -> none  [gram_columns(): return lax.psum(jnp.dot(left_rows, right_rows.T, precision=PRECISE), 'clu')]
    all_gather x7 -> x0, blocking collectives: 90.1 us -> none  [the longest x2 62.8 us: operate(): gathered = lax.all_gather(charges, 'clu', axis=1, tiled=True)]
    pallas_call x0 -> x1, Pallas kernels: none -> 76.1 us  [shards(): pl.pallas_call(functools.partial(kernel, (n_clu, n_rhs, rows, near_slots,...]
    scatter-add x8 -> x0, other arithmetic: 43.6 us -> none  [the longest x2 12.4 us: near_terms(): summed = summed.at[:, first_index].add(toward_first)]
    another operation x15 -> x0, other arithmetic: 36.2 us -> none  [the longest x9 19.6 us: solve_spd(): jnp.linalg.cholesky(matrix)]
    dot_general x17 -> x0, matrix products: 33.5 us -> none  [the longest x2 13.8 us: near_terms(): jnp.einsum('spq,csq->csp', near_blocks, near_second, preferred_element_ty...]
    gather x8 -> x0, local copies, waits for them, and re-layouts: 9.55 us -> none  [the longest x2 2.81 us: near_terms(): near_first = jnp.take(grid, first_index, axis=1)]
  transfers between devices with their start and end apart: 2 -> 0, of which waited for: 2 -> 0; matrix products, arithmetic and copies ran while one was open for 0% -> 0% of each run, Pallas kernels for 0% -> 0%
where the time goes in v1:
time: 87.1 us; the launch traced here: 86.7 us
  Pallas kernels  76.1 us (87%)
  local copies, waits for them, and re-layouts  8.62 us (10%)
  between operations  1.94 us (2%)
    pallas_call x1, Pallas kernels, shards(): pl.pallas_call(functools.partial(kernel, (n_clu, n_rhs, rows, near_slots,...  76.1 us
    unnamed x18, local copies, waits for them, and re-layouts  8.62 us

profile of v1, /device:TPU:0, one launch (start us, length us, event | category | flops | bytes accessed | tf_op | source)
XLA Modules:
  0.0 86.7 jit_solution(3685885757049422913)
XLA Ops:
  1.9 0.8 copy.14.near_pairs
  2.7 0.8 copy.15.far_pairs
  3.5 0.0 copy-start
  3.5 1.2 %copy-done = bf16[64,32,256]{2,1,0:T(8,128)(2,1)S(1)} copy-done((bf16[64,32,256]{2,1,0:T(8,128)(2,1)S(1)}, bf16[64,32,256]{2,1,0:T(8,128)(2,1)}, u32[]{:S(2)}) %copy-start) | copy-done | bytes 1048600
  4.7 0.0 copy-start.1
  4.7 1.2 %copy-done.1 = bf16[64,32,256]{2,1,0:T(8,128)(2,1)S(1)} copy-done((bf16[64,32,256]{2,1,0:T(8,128)(2,1)S(1)}, bf16[64,32,256]{2,1,0:T(8,128)(2,1)}, u32[]{:S(2)}) %copy-start.1) | copy-done | bytes 1048600
  5.9 0.0 copy-start.2
  5.9 0.8 copy-done.2
  6.7 0.0 copy-start.3
  6.7 0.7 copy-done.3
  7.4 0.0 copy-start.4
  7.4 0.7 copy-done.4
  8.0 0.0 copy-start.5
  8.0 0.7 copy-done.5
  8.7 0.0 copy-start.6
  8.7 0.7 copy-done.6
  9.3 76.1 %block_cg.1 = (f32[16,512]{1,0:T(8,128)S(1)}, f32[16,512]{1,0:T(8,128)S(1)}) custom-call(f32[16,512]{1,0:T(8,128)S(1)} %copy-done.2, f32[1,512]{1,0:T(1,128)S(1)} %bitcast.5, s32[64,2]{1,0:T(8,128)S(1)} %copy.14.near_pairs, f32[64]{0:T(128)S(1)} %copy-done.4, s32[1]{0:T(128)S(6)} %copy.18.near_count, s32[64,2]{1,0:T(8,128)S(1)} %copy.15.far_pairs, ...), custom_call_target="tpu_custom_call" | custom-call | tf_op jit(solution)/shard_map/block_cg/pallas_call | solution.py:444
  85.5 0.6 copy.20
  86.1 0.6 copy.21
Async XLA Ops:
  3.5 1.2 %copy-start = (bf16[64,32,256]{2,1,0:T(8,128)(2,1)S(1)}, bf16[64,32,256]{2,1,0:T(8,128)(2,1)}, u32[]{:S(2)}) copy-start(bf16[64,32,256]{2,1,0:T(8,128)(2,1)} %param.19) | copy-start | bytes 3145732
  4.7 1.2 %copy-start.1 = (bf16[64,32,256]{2,1,0:T(8,128)(2,1)S(1)}, bf16[64,32,256]{2,1,0:T(8,128)(2,1)}, u32[]{:S(2)}) copy-start(bf16[64,32,256]{2,1,0:T(8,128)(2,1)} %param.20) | copy-start | bytes 3145732
  5.9 0.8 copy-start.2
  6.7 0.7 copy-start.3
  7.4 0.7 copy-start.4
  8.0 0.7 copy-start.5
  8.7 0.7 copy-start.6

commit v2 on v1

--- a/solution.py
+++ b/solution.py
@@ -33,11 +33,21 @@
 
     def block(_, current):
         current = list(current)
-        for k in range(step):
+        for k in range(0, step, 2):
             for at, m in enumerate(current):
-                column = m[:, k : k + 1]
-                row = m[k : k + 1, :] * (1.0 / m[k : k + 1, k : k + 1])
-                current[at] = jnp.where(row_at == k, row, m - column * row)
+                left = jnp.broadcast_to(m[:, k : k + 1], m.shape)
+                right = jnp.broadcast_to(m[:, k + 1 : k + 2], m.shape)
+                upper, lower = m[k : k + 1, :], m[k + 1 : k + 2, :]
+                turn = 1.0 / left[k : k + 1, :]
+                ratio = left[k + 1 : k + 2, :] * turn
+                corner = right[k : k + 1, :]
+                second = (lower - ratio * upper) * (
+                    1.0 / (right[k + 1 : k + 2, :] - ratio * corner)
+                )
+                first = (upper - corner * second) * turn
+                rest = m - left * first - right * second
+                rest = jnp.where(row_at == k, first, rest)
+                current[at] = jnp.where(row_at == k + 1, second, rest)
         return tuple(
             pltpu.roll(jnp.concatenate([m[step:], m[:step]], axis=0), wide - step, 1)
             for m in current
@@ -49,6 +59,20 @@
 
 def kernel(
     sizes,
+    right_hbm,
+    self_hbm,
+    near_pairs_hbm,
+    near_scale_hbm,
+    near_count_hbm,
+    far_pairs_hbm,
+    far_scale_hbm,
+    far_rank_hbm,
+    far_count_hbm,
+    near_hbm,
+    left_hbm,
+    rightf_hbm,
+    solution_ref,
+    residual_ref,
     right_ref,
     self_ref,
     near_pairs,
@@ -58,11 +82,6 @@
     far_scale,
     far_rank,
     far_count,
-    near_hbm,
-    left_hbm,
-    rightf_hbm,
-    solution_ref,
-    residual_ref,
     near,
     far_l,
     far_r,
@@ -82,6 +101,7 @@
     all_residual,
     grams,
     first_solution,
+    small_sem,
     load_sem,
     clu_send,
     clu_recv,
@@ -98,6 +118,25 @@
     tiles = far_slots // slots_tile
     group = 4
 
+    small = [
+        pltpu.make_async_copy(src, dst, small_sem.at[k])
+        for k, (src, dst) in enumerate(
+            (
+                (right_hbm, right_ref),
+                (self_hbm, self_ref),
+                (near_pairs_hbm, near_pairs),
+                (near_scale_hbm, near_scale),
+                (near_count_hbm, near_count),
+                (far_pairs_hbm, far_pairs),
+                (far_scale_hbm, far_scale),
+                (far_rank_hbm, far_rank),
+                (far_count_hbm, far_count),
+            )
+        )
+    ]
+    for load in small:
+        load.start()
+
     def near_load(g):
         part = pl.ds(g * (near_slots // group), near_slots // group)
         return pltpu.make_async_copy(near_hbm.at[part], near.at[part], load_sem.at[2 + g])
@@ -183,6 +222,7 @@
             1, n_clu, lambda k, total: total + slabs[which, k], slabs[which, 0]
         )
 
+    small[0].wait()
     field = right_ref[...]
     set_charges(0, field)
     all_right[own] = field
@@ -190,6 +230,9 @@
     start_all(grid_copy, 0)
     rhs_start(0, all_right)
 
+    for load in small[1:]:
+        load.wait()
+
     lane = lax.broadcasted_iota(jnp.int32, (1, 128), 1)
     slot_in = lane // rank
     live = far_count[0]
@@ -203,8 +246,8 @@
                 out = jnp.where(slot_in == q, value(g * per + q), out)
             return out
 
-        meta_i[:, at] = spread(lambda s: far_pairs[s, 0])
-        meta_j[:, at] = spread(lambda s: far_pairs[s, 1])
+        meta_i[:, at] = spread(lambda s: far_pairs[0, s])
+        meta_j[:, at] = spread(lambda s: far_pairs[1, s])
         meta_keep[:, at] = jnp.where(
             lane - slot_in * rank < spread(lambda s: far_rank[s]), 1.0, 0.0
         )
@@ -294,7 +337,7 @@
             carry = list(carry)
             for u in range(unroll):
                 s = g * unroll + u
-                i, j = near_pairs[s, 0], near_pairs[s, 1]
+                i, j = near_pairs[0, s], near_pairs[1, s]
                 weight = jnp.where(s < near_live, near_scale[s], jnp.zeros((), F32))
                 block = near[s]
                 offset = j - 2 * me + 2
@@ -438,15 +481,23 @@
     count = rows * n_rhs
     far_rows = far_slots * rank
     vmem = pl.BlockSpec(memory_space=pltpu.VMEM)
-    smem = pl.BlockSpec(memory_space=pltpu.SMEM)
-    anywhere = pl.BlockSpec(memory_space=pl.ANY)
+    hbm = pl.BlockSpec(memory_space=pltpu.HBM)
     field = jax.ShapeDtypeStruct((rows, width), F32)
     return pl.pallas_call(
         functools.partial(kernel, (n_clu, n_rhs, rows, near_slots, far_slots, rank)),
         out_shape=(field, field),
-        in_specs=[vmem, vmem] + [smem] * 7 + [anywhere] * 3,
+        in_specs=[hbm] * 12,
         out_specs=(vmem, vmem),
         scratch_shapes=[
+            pltpu.VMEM((rows, width), F32),
+            pltpu.VMEM((1, width), F32),
+            pltpu.SMEM((2, near_slots), jnp.int32),
+            pltpu.SMEM((near_slots,), F32),
+            pltpu.SMEM((1,), jnp.int32),
+            pltpu.SMEM((2, far_slots), jnp.int32),
+            pltpu.SMEM((far_slots,), F32),
+            pltpu.SMEM((far_slots,), jnp.int32),
+            pltpu.SMEM((1,), jnp.int32),
             pltpu.VMEM(near_blocks.shape, BF16),
             pltpu.VMEM((far_rows, CLUSTER), BF16),
             pltpu.VMEM((far_rows, CLUSTER), BF16),
@@ -466,6 +517,7 @@
             pltpu.VMEM((count, width), F32),
             pltpu.VMEM((2, count, 256), F32),
             pltpu.VMEM((count, width), F32),
+            pltpu.SemaphoreType.DMA((9,)),
             pltpu.SemaphoreType.DMA((6,)),
             pltpu.SemaphoreType.DMA((8, n_clu)),
             pltpu.SemaphoreType.DMA((8, n_clu)),
@@ -473,16 +525,16 @@
             pltpu.SemaphoreType.DMA((5, n_rhs)),
         ],
         compiler_params=pltpu.CompilerParams(
-            collective_id=0, has_side_effects=True, vmem_limit_bytes=48 * 1024 * 1024
+            collective_id=0, has_side_effects=True, vmem_limit_bytes=64 * 1024 * 1024
         ),
         name="block_cg",
     )(
         right_side,
         self_term.reshape(1, width),
-        near_pairs,
+        near_pairs.T,
         near_scale,
         near_count,
-        far_pairs,
+        far_pairs.T,
         far_scale,
         far_rank,
         far_count,

time: 87.1 us -> 76.3 us (0.88)
  local copies, waits for them, and re-layouts: 8.62 us -> 2.75 us
  Pallas kernels: 76.1 us -> 71.4 us
    unnamed x18 -> x2, local copies, waits for them, and re-layouts: 8.62 us -> 2.75 us
    pallas_call x1, Pallas kernels: 76.1 us -> 71.4 us  [shards(): pl.pallas_call(functools.partial(kernel, (n_clu, n_rhs, rows, near_slots,...]
where the time goes in v2:
time: 76.3 us; the launch traced here: 76.1 us
  Pallas kernels  71.4 us (94%)
  local copies, waits for them, and re-layouts  2.75 us (4%)
  between operations  1.93 us (3%)
    pallas_call x1, Pallas kernels, shards(): pl.pallas_call(functools.partial(kernel, (n_clu, n_rhs, rows, near_slots,...  71.4 us
    unnamed x2, local copies, waits for them, and re-layouts  2.75 us

profile of v2, /device:TPU:0, one launch (start us, length us, event | category | flops | bytes accessed | tf_op | source)
XLA Modules:
  0.0 76.1 jit_solution(8967389623812221173)
XLA Ops:
  1.9 71.4 %block_cg.1 = (f32[16,512]{1,0:T(8,128)}, f32[16,512]{1,0:T(8,128)}) custom-call(f32[16,512]{1,0:T(8,128)} %right_hbm.1, f32[1,512]{1,0:T(1,128)} %bitcast.7, s32[2,64]{1,0:T(2,128)} %bitcast.8, f32[64]{0:T(128)} %near_scale_hbm.1, s32[1]{0:T(128)S(6)} %copy.16.near_count_hbm, s32[2,64]{1,0:T(2,128)} %bitcast.9, f32[64]{0:T(128)} %far_scale_hbm.1, ...), custom_call_target="tpu_custom_call" | custom-call | tf_op jit(solution)/shard_map/block_cg/pallas_call | solution.py:486
  73.3 1.4 %copy.18 = f32[16,512]{1,0:T(8,128)} copy(f32[16,512]{1,0:T(8,128)} %get-tuple-element.4) | data formatting | bytes 65536
  74.7 1.4 %copy.19 = f32[16,512]{1,0:T(8,128)} copy(f32[16,512]{1,0:T(8,128)} %get-tuple-element.5) | data formatting | bytes 65536

commit v3 on v2

--- a/solution.py
+++ b/solution.py
@@ -28,7 +28,7 @@
 
 def solve_many(systems):
     size, wide = systems[0].shape
-    step = 8
+    step = 32
     row_at = lax.broadcasted_iota(jnp.int32, (size, 1), 0)
 
     def block(_, current):
@@ -330,7 +330,7 @@
                 it, pl.ds(base, 2 * rows)
             ].astype(F32)
         near_live = near_count[0]
-        unroll = 4
+        unroll = 16
         zero = jnp.zeros((rows, CLUSTER), F32)
 
         def near_slots_step(g, carry):

time: 76.3 us -> 72.3 us (0.948)
  Pallas kernels: 71.4 us -> 67.4 us
    pallas_call x1, Pallas kernels: 71.4 us -> 67.4 us  [shards(): pl.pallas_call(functools.partial(kernel, (n_clu, n_rhs, rows, near_slots,...]
where the time goes in v3:
time: 72.3 us; the launch traced here: 72.1 us
  Pallas kernels  67.4 us (93%)
  local copies, waits for them, and re-layouts  2.75 us (4%)
  between operations  1.93 us (3%)
    pallas_call x1, Pallas kernels, shards(): pl.pallas_call(functools.partial(kernel, (n_clu, n_rhs, rows, near_slots,...  67.4 us
    unnamed x2, local copies, waits for them, and re-layouts  2.75 us

profile of v3, /device:TPU:0, one launch (start us, length us, event | category | flops | bytes accessed | tf_op | source)
XLA Modules:
  0.0 72.1 jit_solution(3061059753527131437)
XLA Ops:
  1.9 67.4 %block_cg.1 = (f32[16,512]{1,0:T(8,128)}, f32[16,512]{1,0:T(8,128)}) custom-call(f32[16,512]{1,0:T(8,128)} %right_hbm.1, f32[1,512]{1,0:T(1,128)} %bitcast.7, s32[2,64]{1,0:T(2,128)} %bitcast.8, f32[64]{0:T(128)} %near_scale_hbm.1, s32[1]{0:T(128)S(6)} %copy.16.near_count_hbm, s32[2,64]{1,0:T(2,128)} %bitcast.9, f32[64]{0:T(128)} %far_scale_hbm.1, ...), custom_call_target="tpu_custom_call" | custom-call | tf_op jit(solution)/shard_map/block_cg/pallas_call | solution.py:486
  69.3 1.4 %copy.18 = f32[16,512]{1,0:T(8,128)} copy(f32[16,512]{1,0:T(8,128)} %get-tuple-element.4) | data formatting | bytes 65536
  70.7 1.4 %copy.19 = f32[16,512]{1,0:T(8,128)} copy(f32[16,512]{1,0:T(8,128)} %get-tuple-element.5) | data formatting | bytes 65536

commit v4 on v3

--- a/solution.py
+++ b/solution.py
@@ -116,7 +116,7 @@
     tile = 256
     slots_tile = tile // rank
     tiles = far_slots // slots_tile
-    group = 4
+    group = 2
 
     small = [
         pltpu.make_async_copy(src, dst, small_sem.at[k])
@@ -330,7 +330,7 @@
                 it, pl.ds(base, 2 * rows)
             ].astype(F32)
         near_live = near_count[0]
-        unroll = 16
+        unroll = 32
         zero = jnp.zeros((rows, CLUSTER), F32)
 
         def near_slots_step(g, carry):

time: 72.3 us -> 72.1 us (level)
  no operation moved by 1% of the time
where the time goes in v4:
time: 72.1 us; the launch traced here: 71.8 us
  Pallas kernels  67.1 us (93%)
  local copies, waits for them, and re-layouts  2.75 us (4%)
  between operations  1.93 us (3%)
    pallas_call x1, Pallas kernels, shards(): pl.pallas_call(functools.partial(kernel, (n_clu, n_rhs, rows, near_slots,...  67.1 us
    unnamed x2, local copies, waits for them, and re-layouts  2.75 us

profile of v4, /device:TPU:0, one launch (start us, length us, event | category | flops | bytes accessed | tf_op | source)
XLA Modules:
  0.0 71.8 jit_solution(7567536644448133565)
XLA Ops:
  1.9 67.1 %block_cg.1 = (f32[16,512]{1,0:T(8,128)}, f32[16,512]{1,0:T(8,128)}) custom-call(f32[16,512]{1,0:T(8,128)} %right_hbm.1, f32[1,512]{1,0:T(1,128)} %bitcast.7, s32[2,64]{1,0:T(2,128)} %bitcast.8, f32[64]{0:T(128)} %near_scale_hbm.1, s32[1]{0:T(128)S(6)} %copy.16.near_count_hbm, s32[2,64]{1,0:T(2,128)} %bitcast.9, f32[64]{0:T(128)} %far_scale_hbm.1, ...), custom_call_target="tpu_custom_call" | custom-call | tf_op jit(solution)/shard_map/block_cg/pallas_call | solution.py:486
  69.1 1.4 %copy.18 = f32[16,512]{1,0:T(8,128)} copy(f32[16,512]{1,0:T(8,128)} %get-tuple-element.4) | data formatting | bytes 65536
  70.4 1.4 %copy.19 = f32[16,512]{1,0:T(8,128)} copy(f32[16,512]{1,0:T(8,128)} %get-tuple-element.5) | data formatting | bytes 65536
